TPU v7x, 32 devices: a whole 2x2x4 slice. The times are simulated.
32 devices in a mesh: blk: 8 (over z, y), shard: 4 (over x, core).
Axes of the slice: x: 2, y: 2, z: 4, core: 2. Of those that a mesh axis runs over, the one named last changes fastest.
Arguments:
- weights: bfloat16 [8, 2, 5120, 5120], P('blk', None, 'shard'), may hold values from -35 to 35
- q_warm: bfloat16 [8, 2, 8, 5120], P('blk'), may hold values from -6 to 6
Outputs:
- new_weights: bfloat16 [8, 2, 5120, 5120], P('blk', None, 'shard')
- q_next: bfloat16 [8, 2, 8, 5120], P('blk')
All inputs are finite; a program needn't handle non-finite values.
Results may differ from a plain program's by a relative error of at most 0.0046.
Values may be sent and summed in bfloat16 or wider, within the bound.
A program may use at most 256 MiB of HBM per device.

v0:
```python
import jax
import jax.numpy as jnp
from jax import lax
from jax.sharding import PartitionSpec as P


def from_behind(block, axis, distance):
    devices = range(lax.axis_size(axis))
    route = [((i - distance) % len(devices), i) for i in devices]
    return lax.ppermute(block, axis, route)


def cholesky_rows(factor):
    gram = jnp.einsum("emkr,emjr->emkj", factor, factor, precision=lax.Precision.HIGHEST)
    gram = lax.psum(gram, "shard")
    lower_tri = jnp.linalg.cholesky(gram)
    result_rows = []
    for position in range(factor.shape[2]):
        current = factor[:, :, position, :]
        for earlier in range(position):
            current = current - lower_tri[:, :, position, earlier][..., None] * result_rows[earlier]
        result_rows.append(current / lower_tri[:, :, position, position][..., None])
    return jnp.stack(result_rows, axis=2)


def per_device(weights, q_warm):
    matrix = weights[0]
    right_start = q_warm[0]
    left_start = from_behind(q_warm, "blk", 1)[0]
    a_right = jnp.einsum("mkc,mrc->mkr", right_start, matrix, preferred_element_type=jnp.float32)
    a_left = jnp.einsum("mkc,mrc->mkr", left_start, matrix, preferred_element_type=jnp.float32)
    from_next = from_behind(a_left, "blk", -1)
    from_previous = from_behind(a_right, "blk", 1)
    factor = jnp.stack([a_right - from_next, from_previous - a_left])
    ortho_rows = cholesky_rows(factor)
    narrow_rows = ortho_rows.astype(jnp.bfloat16)
    partial_cols = jnp.einsum(
        "emkr,mrc->emkc", narrow_rows, matrix, preferred_element_type=jnp.float32
    )
    totals = lax.psum(partial_cols, "shard")
    left_next = from_behind(totals[1], "blk", -1)
    right_previous = from_behind(totals[0].astype(jnp.bfloat16), "blk", 1).astype(jnp.float32)
    columns = jnp.stack([totals[0] - left_next, right_previous - totals[1]])
    correction = jnp.einsum(
        "mkr,mkc->mrc", ortho_rows[1], columns[1], precision=lax.Precision.HIGHEST
    )
    correction = correction - jnp.einsum(
        "mkr,mkc->mrc", ortho_rows[0], columns[0], precision=lax.Precision.HIGHEST
    )
    new_weights = (matrix.astype(jnp.float32) + 0.5 * correction).astype(jnp.bfloat16)
    return (new_weights[None], columns[0].astype(jnp.bfloat16)[None])


def solution(mesh):
    placed = (P("blk", None, "shard", None), P("blk", None, None, None))
    return jax.shard_map(
        per_device,
        mesh=mesh,
        in_specs=placed,
        out_specs=(P("blk", None, "shard", None), P("blk", None, None, None)),
        check_vma=False,
    )
```

profile of v0, /device:TPU:0, one launch (start us, length us, event | category | flops | bytes accessed | tf_op | source)
XLA Modules:
  0.0 224.2 jit_solution(4548000792946363887)
XLA Ops:
  7.2 0.0 all-reduce.2.cloned.1.call-start
  7.2 3.0 %collective-permute-start = (bf16[1,2,8,5120]{3,2,1,0:T(8,128)(2,1)}, bf16[1,2,8,5120]{3,2,1,0:T(8,128)(2,1)S(1)}, u32[]{:S(2)}, u32[]{:S(2)}) collective-permute-start(bf16[1,2,8,5120]{3,2,1,0:T(8,128)(2,1)} %param.3), channel_id=1, source_target_pairs={{28,0},{0,4},{4,8},{8,12},{12,16},{16,20},{20,24},{24,28},{29,1},{... | collective-permute-start | bytes 491528 | tf_op jit(solution)/shard_map/ppermute | solution.py:10
  10.2 12.0 %fusion.4 = f32[2,8,1280]{2,1,0:T(8,128)S(1)} fusion(bf16[1,2,1280,5120]{3,2,1,0:T(8,128)(2,1)} %param.2, bf16[1,2,8,5120]{3,2,1,0:T(8,128)(2,1)} %param.3), kind=kOutput, calls=%fused_computation.5 | convolution fusion | flops 209715200 | bytes 26460160 | tf_op jit(solution)/shard_map/mkc,mrc->mkr/dot_general | solution.py:30
  22.3 1.5 collective-permute-start.2
  23.8 0.0 collective-permute-done
  23.8 11.9 %fusion.2 = f32[2,8,1280]{2,1,0:T(8,128)S(1)} fusion(bf16[1,2,1280,5120]{3,2,1,0:T(8,128)(2,1)} %param.2, bf16[1,2,8,5120]{3,2,1,0:T(8,128)(2,1)S(1)} %collective-permute-done), kind=kOutput, calls=%fused_computation.3 | convolution fusion | flops 209715200 | bytes 26460160 | tf_op jit(solution)/shard_map/mkc,mrc->mkr/dot_general | solution.py:31
  35.7 3.2 %collective-permute-start.1 = (f32[2,8,1280]{2,1,0:T(8,128)S(1)}, f32[2,8,1280]{2,1,0:T(8,128)S(1)}, u32[]{:S(2)}, u32[]{:S(2)}) collective-permute-start(f32[2,8,1280]{2,1,0:T(8,128)S(1)} %fusion.2), channel_id=1, source_target_pairs={{4,0},{8,4},{12,8},{16,12},{20,16},{24,20},{28,24},{0,28},{5,1},{9... | collective-permute-start | bytes 245768 | tf_op jit(solution)/shard_map/ppermute | solution.py:10
  39.0 0.0 collective-permute-done.2
  39.0 2.0 collective-permute-done.1
  41.0 0.3 fusion.14
  41.4 10.1 %psum.14 = f32[2,2,8,8]{2,3,1,0:T(8,128)S(1)} all-reduce(f32[2,2,8,8]{2,3,1,0:T(8,128)S(1)} %fusion.14), channel_id=1, replica_groups=mesh['blk'=8,'shard'=4] {'shard'}, use_global_device_ids=true, to_apply=%region_0.0 | all-reduce | flops 256 | bytes 2048 | tf_op jit(solution)/shard_map/psum | solution.py:15
  51.5 0.1 copy.13
  51.6 2.9 %custom-call.4 = f32[2,2,8,8]{3,2,1,0:T(8,128)S(1)} custom-call(f32[2,2,8,8]{3,2,1,0:T(8,128)S(1)} %fusion.37), custom_call_target="Cholesky" | custom-call | tf_op jit(solution)/shard_map/jit(cholesky)/cholesky | solution.py:16
  54.5 0.1 select_reduce_fusion
  54.5 0.2 compare_reduce_fusion
  54.7 0.1 select_select_fusion
  54.8 0.3 slice_reduce_fusion.20
  55.1 0.3 slice_reduce_fusion.7
  55.4 0.6 subtract_divide_fusion
  56.0 0.3 stack.11
  56.3 11.2 %fusion.7 = f32[2,2,8,5120]{3,2,0,1:T(8,128)} fusion(bf16[1,2,1280,5120]{3,2,1,0:T(8,128)(2,1)} %param.2, f32[2,2,8,1280]{3,2,1,0:T(8,128)S(1)} %stack.11), kind=kOutput, calls=%fused_computation.8 | convolution fusion | flops 419471360 | bytes 27033600 | tf_op jit(solution)/shard_map/emkr,mrc->emkc/dot_general | solution.py:37
  67.4 0.0 all-reduce.2.cloned.1.call-update
  67.5 35.8 %all-reduce.2.cloned.1.call-done = f32[2,2,8,5120]{3,2,0,1:T(8,128)} async-done(((f32[2,2,8,5120]{3,2,0,1:T(8,128)}), f32[2,2,8,5120]{3,2,0,1:T(8,128)}) %all-reduce.2.cloned.1.call-update) | async-done | bytes 655376 | tf_op jit(solution)/shard_map/psum | solution.py:40
  103.3 1.0 slice_bitcast_fusion
  104.3 4.3 %collective-permute-start.4 = (f32[2,8,5120]{2,1,0:T(8,128)S(1)}, f32[2,8,5120]{2,1,0:T(8,128)S(1)}, u32[]{:S(2)}, u32[]{:S(2)}) collective-permute-start(f32[2,8,5120]{2,1,0:T(8,128)S(1)} %slice_bitcast_fusion), channel_id=1, source_target_pairs={{4,0},{8,4},{12,8},{16,12},{20,16},{24,20},{28,24},{0,28},{5,1},{9... | collective-permute-start | bytes 983048 | tf_op jit(solution)/shard_map/ppermute | solution.py:10
  108.6 1.0 fusion.13
  109.6 0.2 collective-permute-start.3
  109.8 4.8 %collective-permute-done.4 = f32[2,8,5120]{2,1,0:T(8,128)S(1)} collective-permute-done((f32[2,8,5120]{2,1,0:T(8,128)S(1)}, f32[2,8,5120]{2,1,0:T(8,128)S(1)}, u32[]{:S(2)}, u32[]{:S(2)}) %collective-permute-start.4) | collective-permute-done | bytes 327712 | tf_op jit(solution)/shard_map/ppermute | solution.py:10
  114.6 46.6 %fusion.17 = f32[2,1280,5120]{2,1,0:T(8,128)} fusion(f32[2,8,5120]{2,1,0:T(8,128)S(1)} %collective-permute-done.4, f32[2,2,8,5120]{3,2,0,1:T(8,128)} %all-reduce.2.cloned.1.call-done, f32[2,2,8,1280]{3,2,1,0:T(8,128)S(1)} %stack.11), kind=kOutput, calls=%fused_computation.36 | convolution fusion | flops 1258373120 | bytes 53166080 | tf_op jit(solution)/shard_map/mkr,mkc->mrc/dot_general | solution.py:47
  161.2 0.7 convert_bitcast_fusion
  161.9 0.0 collective-permute-done.3
  161.9 55.4 %fusion.6 = bf16[1,2,1280,5120]{3,2,1,0:T(8,128)(2,1)} fusion(f32[2,1280,5120]{2,1,0:T(8,128)} %fusion.17, bf16[1,2,1280,5120]{3,2,1,0:T(8,128)(2,1)} %param.2, bf16[2,8,5120]{2,1,0:T(8,128)(2,1)S(1)} %collective-permute-done.3, f32[2,2,8,1280]{3,2,1,0:T(8,128)S(1)} %stack.11, f32[2,2,8,5120]{3,2,0,1:T(8,128)S(1)} %copy-done), kind=kOutput, calls=%fused_computation.7 | convolution fusion | flops 1323991040 | bytes 105431040 | tf_op jit(solution)/shard_map/mkr,mkc->mrc/dot_general | solution.py:44
  (7 shorter events, 0.0 us)
Async XLA Ops:
  7.2 96.1 %all-reduce.2.cloned.1.call-start = ((), (), s32[]{:S(2)}) async-start(), calls=%async_computation | async-start | bytes 1310720 | tf_op jit(solution)/shard_map/psum | solution.py:40
  7.2 16.6 %collective-permute-start = (bf16[1,2,8,5120]{3,2,1,0:T(8,128)(2,1)}, bf16[1,2,8,5120]{3,2,1,0:T(8,128)(2,1)S(1)}, u32[]{:S(2)}, u32[]{:S(2)}) collective-permute-start(bf16[1,2,8,5120]{3,2,1,0:T(8,128)(2,1)} %param.3), channel_id=1, source_target_pairs={{28,0},{0,4},{4,8},{8,12},{12,16},{16,20},{20,24},{24,28},{29,1},{... | collective-permute-start | bytes 491528 | tf_op jit(solution)/shard_map/ppermute | solution.py:10
  22.3 16.7 %collective-permute-start.2 = (f32[2,8,1280]{2,1,0:T(8,128)S(1)}, f32[2,8,1280]{2,1,0:T(8,128)S(1)}, u32[]{:S(2)}, u32[]{:S(2)}) collective-permute-start(f32[2,8,1280]{2,1,0:T(8,128)S(1)} %fusion.4), channel_id=1, source_target_pairs={{28,0},{0,4},{4,8},{8,12},{12,16},{16,20},{20,24},{24,28},{29,1},{... | collective-permute-start | bytes 245768 | tf_op jit(solution)/shard_map/ppermute | solution.py:10
  35.7 5.3 %collective-permute-start.1 = (f32[2,8,1280]{2,1,0:T(8,128)S(1)}, f32[2,8,1280]{2,1,0:T(8,128)S(1)}, u32[]{:S(2)}, u32[]{:S(2)}) collective-permute-start(f32[2,8,1280]{2,1,0:T(8,128)S(1)} %fusion.2), channel_id=1, source_target_pairs={{4,0},{8,4},{12,8},{16,12},{20,16},{24,20},{28,24},{0,28},{5,1},{9... | collective-permute-start | bytes 245768 | tf_op jit(solution)/shard_map/ppermute | solution.py:10
  104.3 10.3 %collective-permute-start.4 = (f32[2,8,5120]{2,1,0:T(8,128)S(1)}, f32[2,8,5120]{2,1,0:T(8,128)S(1)}, u32[]{:S(2)}, u32[]{:S(2)}) collective-permute-start(f32[2,8,5120]{2,1,0:T(8,128)S(1)} %slice_bitcast_fusion), channel_id=1, source_target_pairs={{4,0},{8,4},{12,8},{16,12},{20,16},{24,20},{28,24},{0,28},{5,1},{9... | collective-permute-start | bytes 983048 | tf_op jit(solution)/shard_map/ppermute | solution.py:10
  109.6 51.6 %copy-start = (f32[2,2,8,5120]{3,2,0,1:T(8,128)S(1)}, f32[2,2,8,5120]{3,2,0,1:T(8,128)}, u32[]{:S(2)}) copy-start(f32[2,2,8,5120]{3,2,0,1:T(8,128)} %all-reduce.2.cloned.1.call-done) | copy-start | bytes 1966084
  109.6 52.3 %collective-permute-start.3 = (bf16[2,8,5120]{2,1,0:T(8,128)(2,1)S(1)}, bf16[2,8,5120]{2,1,0:T(8,128)(2,1)S(1)}, u32[]{:S(2)}, u32[]{:S(2)}) collective-permute-start(bf16[2,8,5120]{2,1,0:T(8,128)(2,1)S(1)} %fusion.13), channel_id=1, source_target_pairs={{28,0},{0,4},{4,8},{8,12},{12,16},{16,20},{20,24},{24,28},{29,1},{... | collective-permute-start | bytes 491528 | tf_op jit(solution)/shard_map/ppermute | solution.py:10
Sparse Core Ops, SparseCore 0:
  67.6 35.6 all-reduce.1
where the time goes:
time: 225 us; the launch traced here: 224 us
  matrix products  137 us (61%)
  waiting for transfers between devices  42.7 us (19%)
  between operations  14.1 us (6%)
  starting transfers between devices  12.3 us (5%)
  blocking collectives  10.1 us (4%)
  other arithmetic  4.55 us (2%)
  local copies, waits for them, and re-layouts  2.93 us (1%)
    dot_general x1, matrix products, per_device(): jnp.einsum('mkr,mkc->mrc', ortho_rows[1], columns[1], precision=lax.Preci...  55.4 us
    dot_general x1, matrix products, per_device(): jnp.einsum('mkr,mkc->mrc', ortho_rows[0], columns[0], precision=lax.Preci...  46.6 us
    psum x1, waiting for transfers between devices, per_device(): totals = lax.psum(partial_cols, 'shard')  35.8 us
    ppermute x5, starting transfers between devices, from_behind(): return lax.ppermute(block, axis, route)  12.3 us
    dot_general x1, matrix products, per_device(): jnp.einsum('mkc,mrc->mkr', right_start, matrix, preferred_element_type=jn...  12 us
    dot_general x1, matrix products, per_device(): jnp.einsum('mkc,mrc->mkr', left_start, matrix, preferred_element_type=jnp...  11.9 us
    dot_general x1, matrix products, per_device(): jnp.einsum('emkr,mrc->emkc', narrow_rows, matrix, preferred_element_type=...  11.2 us
    psum x1, blocking collectives, cholesky_rows(): gram = lax.psum(gram, 'shard')  10.1 us
  transfers between devices with their start and end apart: 6, of which 3 were waited for; matrix products, arithmetic and copies ran while one was open for 32% of the time, Pallas kernels for 0%

commit v1 on v0

v1 whole, which is shorter than its diff:
```python
import functools

import jax
import jax.numpy as jnp
from jax import lax
from jax.experimental import pallas as pl
from jax.experimental.pallas import tpu as pltpu
from jax.sharding import PartitionSpec as P

F32 = jnp.float32
BF16 = jnp.bfloat16
NT = (((1,), (1,)), ((), ()))
NN = (((1,), (0,)), ((), ()))
TN = (((0,), (0,)), ((), ()))


def factors_kernel(
    nb, ns, mats, rank, rows, width, chunk,
    q_ref, w_ref,
    h_ref, c_ref,
    w_v, q_in, qq, a_v, ar_in, al_in, p_v, g_out, g_in, hb,
    x_out, x_in, y_out, z_in, t_v, tr_in, tl_in, c_all,
    w_sem, q_sem, a_sem, g_ssem, g_rsem, x_sem, z_sem, t_sem, c_ssem, c_rsem,
):
    b, s = lax.axis_index("blk"), lax.axis_index("shard")
    nxt, prv = lax.rem(b + 1, nb), lax.rem(b + nb - 1, nb)
    core = lax.rem(s, 2)
    mine = s // 2
    other = mine * 2 + (1 - core)
    nr = ns // 2
    part = width // ns
    pieces = rows // chunk

    loads = []
    for m in range(mats):
        for t in range(pieces):
            where = pl.ds(t * chunk, chunk)
            load = pltpu.make_async_copy(
                w_ref.at[0, m, where, :], w_v.at[m, where, :], w_sem.at[m, t]
            )
            load.start()
            loads.append(load)

    barrier = pltpu.get_barrier_semaphore()
    partners = [(nxt, s), (prv, s)]
    partners += [(b, lax.rem(s + d, ns)) for d in range(1, ns)]
    for partner in partners:
        pl.semaphore_signal(
            barrier, inc=1, device_id=partner, device_id_type=pl.DeviceIdType.MESH
        )
    pl.semaphore_wait(barrier, len(partners))

    sent = []

    def send(src, dst, ssem, rsem, device):
        copy = pltpu.make_async_remote_copy(
            src_ref=src, dst_ref=dst, send_sem=ssem, recv_sem=rsem,
            device_id=device, device_id_type=pl.DeviceIdType.MESH,
        )
        copy.start()
        sent.append(copy)
        return copy

    q_copy = send(q_ref, q_in, q_sem.at[0], q_sem.at[1], (nxt, s))
    q_copy.wait_recv()
    own_q = q_ref[...].astype(F32)
    far_q = q_in[...].astype(F32)
    for m in range(mats):
        low, high = m * rank, (m + 1) * rank
        qq[m] = jnp.concatenate([own_q[low:high], far_q[low:high]], axis=0).astype(BF16)

    a_copies = []
    for m in range(mats):
        for t in range(pieces):
            loads[m * pieces + t].wait()
            a_v[m, :, t * chunk:(t + 1) * chunk] = lax.dot_general(
                qq[m], w_v[m, t * chunk:(t + 1) * chunk, :], NT, preferred_element_type=F32
            )
        a_copies.append((
            send(a_v.at[m, 0:rank], ar_in.at[m], a_sem.at[0, m], a_sem.at[1, m], (nxt, s)),
            send(a_v.at[m, rank:2 * rank], al_in.at[m], a_sem.at[2, m], a_sem.at[3, m], (prv, s)),
        ))

    g_copies = []
    for m in range(mats):
        for copy in a_copies[m]:
            copy.wait_recv()
        p = jnp.concatenate(
            [a_v[m, 0:rank] - al_in[m], ar_in[m] - a_v[m, rank:2 * rank]], axis=0
        )
        p_v[m] = p
        g_out[m, :, 0:2 * rank] = lax.dot_general(
            p, p, NT, precision=lax.Precision.HIGHEST, preferred_element_type=F32
        )
        g_copies.append([
            send(
                g_out.at[m], g_in.at[m, d - 1], g_ssem.at[m, d - 1], g_rsem.at[m, d - 1],
                (b, lax.rem(s + d, ns)),
            )
            for d in range(1, ns)
        ])

    def orthonormalize(m):
        for copy in g_copies[m]:
            copy.wait_recv()
        gram = g_out[m]
        for d in range(1, ns):
            gram = gram + g_in[m, d - 1]
        for e in range(2):
            low = e * rank
            left = gram[low:low + rank, low:low + rank]
            right = p_v[m, low:low + rank]
            place = lax.broadcasted_iota(jnp.int32, (rank, 1), 0)
            diagonal = jnp.ones((rank, 1), F32)
            for k in range(rank):
                pivot = left[k:k + 1, k:k + 1]
                diagonal = jnp.where(place == k, pivot, diagonal)
                if k < rank - 1:
                    factor = jnp.where(place > k, left[:, k:k + 1] / pivot, 0.0)
                    left = left - factor * left[k:k + 1]
                    right = right - factor * right[k:k + 1]
            right = right * (1.0 / jnp.sqrt(diagonal))
            p_v[m, low:low + rank] = right
        h = p_v[m]
        hb[m] = h.astype(BF16)
        row = lax.broadcasted_iota(jnp.int32, (2 * rank, 1), 0)
        scaled = h * jnp.where(row < rank, -0.5, 0.5)
        wide = scaled.astype(BF16)
        h_ref[m] = jnp.concatenate([wide, (scaled - wide.astype(F32)).astype(BF16)], axis=0)

    def product(m, owner):
        where = pl.ds(pl.multiple_of(owner * part, 128), part)
        return lax.dot_general(hb[m], w_v[m, :, where], NN, preferred_element_type=F32)

    x_copies, z_copies, t_copies, c_copies = {}, {}, {}, {}

    def for_other_core(m):
        for d in list(range(1, nr)) + [0]:
            group = lax.rem(mine + d, nr)
            x_out[m, d] = product(m, group * 2 + (1 - core))
            x_copies[m, d] = send(
                x_out.at[m, d], x_in.at[m, d], x_sem.at[0, m, d], x_sem.at[1, m, d], (b, other)
            )

    def for_this_core(m):
        for d in range(1, nr):
            group = lax.rem(mine + d, nr)
            own = product(m, group * 2 + core)
            x_copies[m, d].wait_recv()
            y_out[m, d - 1] = own + x_in[m, d]
            z_copies[m, d] = send(
                y_out.at[m, d - 1], z_in.at[m, d - 1],
                z_sem.at[0, m, d - 1], z_sem.at[1, m, d - 1], (b, group * 2 + core),
            )
        own = product(m, s)
        x_copies[m, 0].wait_recv()
        t_v[m] = own + x_in[m, 0]

    def to_neighbours(m):
        total = t_v[m]
        for d in range(1, nr):
            z_copies[m, d].wait_recv()
            total = total + z_in[m, d - 1]
        t_v[m] = total
        t_copies[m] = (
            send(t_v.at[m, 0:rank], tr_in.at[m], t_sem.at[0, m], t_sem.at[1, m], (nxt, s)),
            send(t_v.at[m, rank:2 * rank], tl_in.at[m], t_sem.at[2, m], t_sem.at[3, m], (prv, s)),
        )

    def spread_columns(m):
        for copy in t_copies[m]:
            copy.wait_recv()
        c_all[m, s] = jnp.concatenate(
            [t_v[m, 0:rank] - tl_in[m], tr_in[m] - t_v[m, rank:2 * rank]], axis=0
        ).astype(BF16)
        c_copies[m] = [
            send(
                c_all.at[m, s], c_all.at[m, s], c_ssem.at[m, d - 1], c_rsem.at[m, d - 1],
                (b, lax.rem(s + d, ns)),
            )
            for d in range(1, ns)
        ]

    orthonormalize(0)
    for_other_core(0)
    for_this_core(0)
    for m in range(1, mats):
        orthonormalize(m)
        for_other_core(m)
        to_neighbours(m - 1)
        for_this_core(m)
        spread_columns(m - 1)
    to_neighbours(mats - 1)
    spread_columns(mats - 1)

    for m in range(mats):
        for copy in c_copies[m]:
            copy.wait_recv()
        for owner in range(ns):
            c_ref[m, :, owner * part:(owner + 1) * part] = c_all[m, owner]
    for copy in sent:
        copy.wait_send()


def update_kernel(rank, step, w_ref, h_ref, c_ref, out_ref, q_ref):
    width = w_ref.shape[-1]
    for start in range(0, width, step):
        where = slice(start, start + step)
        cols = c_ref[0, :, where]
        both = jnp.concatenate([cols, cols], axis=0)
        change = lax.dot_general(h_ref[0], both, TN, preferred_element_type=F32)
        out_ref[0, 0, :, where] = (w_ref[0, 0, :, where].astype(F32) + change).astype(BF16)

    @pl.when(pl.program_id(1) == 0)
    def _():
        q_ref[0, 0] = c_ref[0].astype(F32)[0:rank].astype(BF16)


def per_device(nb, ns, weights, q_warm):
    _, mats, rows, width = weights.shape
    rank = q_warm.shape[2]
    chunk = 256 if rows % 256 == 0 else 128
    nr, part = ns // 2, width // ns
    vmem, dma = pltpu.VMEM, pltpu.SemaphoreType.DMA
    whole = pl.BlockSpec(memory_space=pltpu.VMEM)
    flops = 2 * 2 * mats * 2 * rank * rows * width
    h, c = pl.pallas_call(
        functools.partial(factors_kernel, nb, ns, mats, rank, rows, width, chunk),
        out_shape=(
            jax.ShapeDtypeStruct((mats, 4 * rank, rows), BF16),
            jax.ShapeDtypeStruct((mats, 2 * rank, width), BF16),
        ),
        in_specs=[whole, pl.BlockSpec(memory_space=pl.ANY)],
        out_specs=(whole, whole),
        scratch_shapes=[
            vmem((mats, rows, width), BF16),
            vmem((mats * rank, width), BF16),
            vmem((mats, 2 * rank, width), BF16),
            vmem((mats, 2 * rank, rows), F32),
            vmem((mats, rank, rows), F32),
            vmem((mats, rank, rows), F32),
            vmem((mats, 2 * rank, rows), F32),
            vmem((mats, 2 * rank, 128), F32),
            vmem((mats, ns - 1, 2 * rank, 128), F32),
            vmem((mats, 2 * rank, rows), BF16),
            vmem((mats, nr, 2 * rank, part), F32),
            vmem((mats, nr, 2 * rank, part), F32),
            vmem((mats, nr - 1, 2 * rank, part), F32),
            vmem((mats, nr - 1, 2 * rank, part), F32),
            vmem((mats, 2 * rank, part), F32),
            vmem((mats, rank, part), F32),
            vmem((mats, rank, part), F32),
            vmem((mats, ns, 2 * rank, part), BF16),
            dma((mats, rows // chunk)),
            dma((2,)),
            dma((4, mats)),
            dma((mats, ns - 1)),
            dma((mats, ns - 1)),
            dma((2, mats, nr)),
            dma((2, mats, nr - 1)),
            dma((4, mats)),
            dma((mats, ns - 1)),
            dma((mats, ns - 1)),
        ],
        compiler_params=pltpu.CompilerParams(
            collective_id=0, has_side_effects=True, vmem_limit_bytes=50 * 2**20
        ),
        cost_estimate=pl.CostEstimate(
            flops=flops, bytes_accessed=weights.size * 2, transcendentals=0
        ),
        name="factors",
    )(q_warm.reshape(mats * rank, width), weights)
    step = 1280 if width % 1280 == 0 else width
    new_weights, q_next = pl.pallas_call(
        functools.partial(update_kernel, rank, step),
        grid=(mats, rows // chunk),
        out_shape=(
            jax.ShapeDtypeStruct(weights.shape, BF16),
            jax.ShapeDtypeStruct(q_warm.shape, BF16),
        ),
        in_specs=[
            pl.BlockSpec((1, 1, chunk, width), lambda m, t: (0, m, t, 0)),
            pl.BlockSpec((1, 4 * rank, chunk), lambda m, t: (m, 0, t)),
            pl.BlockSpec((1, 2 * rank, width), lambda m, t: (m, 0, 0)),
        ],
        out_specs=(
            pl.BlockSpec((1, 1, chunk, width), lambda m, t: (0, m, t, 0)),
            pl.BlockSpec((1, 1, rank, width), lambda m, t: (0, m, 0, 0)),
        ),
        compiler_params=pltpu.CompilerParams(vmem_limit_bytes=50 * 2**20),
        cost_estimate=pl.CostEstimate(
            flops=flops // 2, bytes_accessed=weights.size * 4, transcendentals=0
        ),
        name="update",
    )(weights, h, c)
    return new_weights, q_next


def solution(mesh):
    placed = (P("blk", None, "shard", None), P("blk", None, None, None))
    return jax.shard_map(
        functools.partial(per_device, mesh.shape["blk"], mesh.shape["shard"]),
        mesh=mesh,
        in_specs=placed,
        out_specs=placed,
        check_vma=False,
    )
```

time: 225 us -> 75.3 us (0.33)
  matrix products: 137 us -> 0 us
  Pallas kernels: 0 us -> 73.4 us
  waiting for transfers between devices: 42.7 us -> 0 us
  between operations: 14.1 us -> 0.65 us
  starting transfers between devices: 12.3 us -> 0 us
  blocking collectives: 10.1 us -> 0 us
  other arithmetic: 4.55 us -> 0 us
    dot_general x6 -> x0, matrix products: 137 us -> none  [the longest x1 55.4 us: per_device(): jnp.einsum('mkr,mkc->mrc', ortho_rows[1], columns[1], precision=lax.Preci...]
    pallas_call x0 -> x2, Pallas kernels: none -> 73.4 us  [the longest x1 50.3 us: per_device(): pl.pallas_call(functools.partial(factors_kernel, nb, ns, mats, rank, rows...]
    psum x1 -> x0, waiting for transfers between devices: 35.8 us -> none  [per_device(): totals = lax.psum(partial_cols, 'shard')]
    ppermute x5 -> x0, starting transfers between devices: 12.3 us -> none  [from_behind(): return lax.ppermute(block, axis, route)]
    psum x1 -> x0, blocking collectives: 10.1 us -> none  [cholesky_rows(): gram = lax.psum(gram, 'shard')]
    ppermute x5 -> x0, waiting for transfers between devices: 6.86 us -> none  [from_behind(): return lax.ppermute(block, axis, route)]
    another operation x6 -> x0, other arithmetic: 3.14 us -> none  [the longest x4 3.11 us: cholesky_rows(): lower_tri = jnp.linalg.cholesky(gram)]
  transfers between devices with their start and end apart: 6 -> 0, of which waited for: 3 -> 0; matrix products, arithmetic and copies ran while one was open for 32% -> 0% of each run, Pallas kernels for 0% -> 0%
where the time goes in v1:
time: 75.3 us; the launch traced here: 75 us
  Pallas kernels  73.4 us (97%)
  local copies, waits for them, and re-layouts  0.91 us (1%)
    pallas_call x1, Pallas kernels, per_device(): pl.pallas_call(functools.partial(factors_kernel, nb, ns, mats, rank, rows...  50.3 us
    pallas_call x1, Pallas kernels, per_device(): pl.pallas_call(functools.partial(update_kernel, rank, step), grid=(mats,...  23.1 us

profile of v1, /device:TPU:0, one launch (start us, length us, event | category | flops | bytes accessed | tf_op | source)
XLA Modules:
  0.0 75.0 jit_solution(1964522169655461382)
XLA Ops:
  0.6 0.0 copy-start
  0.6 0.9 %copy-done = bf16[1,2,8,5120]{3,2,1,0:T(8,128)(2,1)S(1)} copy-done((bf16[1,2,8,5120]{3,2,1,0:T(8,128)(2,1)S(1)}, bf16[1,2,8,5120]{3,2,1,0:T(8,128)(2,1)}, u32[]{:S(2)}) %copy-start) | copy-done | bytes 163864
  1.5 50.3 %factors.1 = (bf16[2,32,1280]{2,1,0:T(8,128)(2,1)S(1)}, bf16[2,16,5120]{2,1,0:T(8,128)(2,1)S(1)}) custom-call(bf16[16,5120]{1,0:T(8,128)(2,1)S(1)} %bitcast.1, bf16[1,2,1280,5120]{3,2,1,0:T(8,128)(2,1)} %w_ref.3), custom_call_target="tpu_custom_call" | custom-call | flops 838860800 | bytes 26214400 | tf_op jit(solution)/shard_map/factors/pallas_call | solution.py:227
  51.8 23.1 %update.1 = (bf16[1,2,1280,5120]{3,2,1,0:T(8,128)(2,1)}, bf16[1,2,8,5120]{3,2,1,0:T(8,128)(2,1)}) custom-call(bf16[1,2,1280,5120]{3,2,1,0:T(8,128)(2,1)} %w_ref.3, bf16[2,32,1280]{2,1,0:T(8,128)(2,1)S(1)} %get-tuple-element.4.h_ref, bf16[2,16,5120]{2,1,0:T(8,128)(2,1)S(1)} %get-tuple-element.5.c_ref), custom_call_target="tpu_custom_call" | custom-call | flops 419430400 | bytes 52428800 | tf_op jit(solution)/shard_map/update/pallas_call | solution.py:274
Async XLA Ops:
  0.6 0.9 %copy-start = (bf16[1,2,8,5120]{3,2,1,0:T(8,128)(2,1)S(1)}, bf16[1,2,8,5120]{3,2,1,0:T(8,128)(2,1)}, u32[]{:S(2)}) copy-start(bf16[1,2,8,5120]{3,2,1,0:T(8,128)(2,1)} %param.3) | copy-start | bytes 491524

commit v2 on v1

--- a/solution.py
+++ b/solution.py
@@ -17,9 +17,9 @@
 def factors_kernel(
     nb, ns, mats, rank, rows, width, chunk,
     q_ref, w_ref,
-    h_ref, c_ref,
-    w_v, q_in, qq, a_v, ar_in, al_in, p_v, g_out, g_in, hb,
-    x_out, x_in, y_out, z_in, t_v, tr_in, tl_in, c_all,
+    h_ref, c_ref, w_v,
+    q_own, q_in, qq, a_v, ar_in, al_in, p_v, g_out, g_in, hb,
+    s_all, x_out, x_in, y_out, z_in, t_v, tr_in, tl_in, c_all,
     w_sem, q_sem, a_sem, g_ssem, g_rsem, x_sem, z_sem, t_sem, c_ssem, c_rsem,
 ):
     b, s = lax.axis_index("blk"), lax.axis_index("shard")
@@ -31,6 +31,8 @@
     part = width // ns
     pieces = rows // chunk
 
+    local_q = pltpu.make_async_copy(q_ref, q_own, q_sem.at[4])
+    local_q.start()
     loads = []
     for m in range(mats):
         for t in range(pieces):
@@ -61,9 +63,15 @@
         sent.append(copy)
         return copy
 
-    q_copy = send(q_ref, q_in, q_sem.at[0], q_sem.at[1], (nxt, s))
-    q_copy.wait_recv()
-    own_q = q_ref[...].astype(F32)
+    local_q.wait()
+    half = pl.ds(pl.multiple_of(core * (width // 2), 128), width // 2)
+    send(
+        q_own.at[:, half], q_in.at[:, half], q_sem.at[0], q_sem.at[1], (nxt, s)
+    ).wait_recv()
+    send(
+        q_in.at[:, half], q_in.at[:, half], q_sem.at[2], q_sem.at[3], (b, other)
+    ).wait_recv()
+    own_q = q_own[...].astype(F32)
     far_q = q_in[...].astype(F32)
     for m in range(mats):
         low, high = m * rank, (m + 1) * rank
@@ -81,8 +89,9 @@
             send(a_v.at[m, rank:2 * rank], al_in.at[m], a_sem.at[2, m], a_sem.at[3, m], (prv, s)),
         ))
 
-    g_copies = []
-    for m in range(mats):
+    g_copies = {}
+
+    def send_gram(m):
         for copy in a_copies[m]:
             copy.wait_recv()
         p = jnp.concatenate(
@@ -92,13 +101,13 @@
         g_out[m, :, 0:2 * rank] = lax.dot_general(
             p, p, NT, precision=lax.Precision.HIGHEST, preferred_element_type=F32
         )
-        g_copies.append([
+        g_copies[m] = [
             send(
                 g_out.at[m], g_in.at[m, d - 1], g_ssem.at[m, d - 1], g_rsem.at[m, d - 1],
                 (b, lax.rem(s + d, ns)),
             )
             for d in range(1, ns)
-        ])
+        ]
 
     def orthonormalize(m):
         for copy in g_copies[m]:
@@ -128,13 +137,24 @@
         wide = scaled.astype(BF16)
         h_ref[m] = jnp.concatenate([wide, (scaled - wide.astype(F32)).astype(BF16)], axis=0)
 
+    def prepare(m):
+        if part % 128:
+            for owner in range(ns):
+                s_all[m, owner] = lax.dot_general(
+                    hb[m], w_v[m, :, owner * part:(owner + 1) * part], NN,
+                    preferred_element_type=F32,
+                )
+
     def product(m, owner):
+        if part % 128:
+            return s_all[m, owner]
         where = pl.ds(pl.multiple_of(owner * part, 128), part)
         return lax.dot_general(hb[m], w_v[m, :, where], NN, preferred_element_type=F32)
 
     x_copies, z_copies, t_copies, c_copies = {}, {}, {}, {}
 
     def for_other_core(m):
+        prepare(m)
         for d in list(range(1, nr)) + [0]:
             group = lax.rem(mine + d, nr)
             x_out[m, d] = product(m, group * 2 + (1 - core))
@@ -181,17 +201,19 @@
             for d in range(1, ns)
         ]
 
+    send_gram(0)
     orthonormalize(0)
     for_other_core(0)
-    for_this_core(0)
     for m in range(1, mats):
+        send_gram(m)
+        for_this_core(m - 1)
         orthonormalize(m)
         for_other_core(m)
         to_neighbours(m - 1)
-        for_this_core(m)
-        spread_columns(m - 1)
+    for_this_core(mats - 1)
     to_neighbours(mats - 1)
-    spread_columns(mats - 1)
+    for m in range(mats):
+        spread_columns(m)
 
     for m in range(mats):
         for copy in c_copies[m]:
@@ -202,38 +224,58 @@
         copy.wait_send()
 
 
-def update_kernel(rank, step, w_ref, h_ref, c_ref, out_ref, q_ref):
-    width = w_ref.shape[-1]
-    for start in range(0, width, step):
-        where = slice(start, start + step)
-        cols = c_ref[0, :, where]
+def update_kernel(rank, chunk, step, w_ref, h_ref, c_ref, out_ref, q_ref, slots, out_sem, q_v, q_sem):
+    mats, rows, width = w_ref.shape
+    count = slots.shape[0]
+    q_copies, copies = [], []
+    for m in range(mats):
+        cols = c_ref[m]
+        q_v[m] = cols.astype(F32)[0:rank].astype(BF16)
+        copy = pltpu.make_async_copy(q_v.at[m], q_ref.at[0, m], q_sem.at[m])
+        copy.start()
+        q_copies.append(copy)
         both = jnp.concatenate([cols, cols], axis=0)
-        change = lax.dot_general(h_ref[0], both, TN, preferred_element_type=F32)
-        out_ref[0, 0, :, where] = (w_ref[0, 0, :, where].astype(F32) + change).astype(BF16)
-
-    @pl.when(pl.program_id(1) == 0)
-    def _():
-        q_ref[0, 0] = c_ref[0].astype(F32)[0:rank].astype(BF16)
+        for first in range(0, rows, chunk):
+            here = slice(first, first + chunk)
+            slot = len(copies) % count
+            if len(copies) >= count:
+                copies[-count].wait()
+            for start in range(0, width, step):
+                where = slice(start, start + step)
+                change = lax.dot_general(
+                    h_ref[m, :, here], both[:, where], TN, preferred_element_type=F32
+                )
+                slots[slot, :, where] = (w_ref[m, here, where].astype(F32) + change).astype(BF16)
+            copy = pltpu.make_async_copy(
+                slots.at[slot], out_ref.at[0, m, pl.ds(first, chunk), :], out_sem.at[slot]
+            )
+            copy.start()
+            copies.append(copy)
+    for copy in copies[-count:] + q_copies:
+        copy.wait()
 
 
 def per_device(nb, ns, weights, q_warm):
     _, mats, rows, width = weights.shape
     rank = q_warm.shape[2]
-    chunk = 256 if rows % 256 == 0 else 128
+    chunk = next(size for size in (256, 128, rows) if rows % size == 0)
+    tile = next(size for size in (128, 64, 16) if rows % size == 0)
     nr, part = ns // 2, width // ns
     vmem, dma = pltpu.VMEM, pltpu.SemaphoreType.DMA
     whole = pl.BlockSpec(memory_space=pltpu.VMEM)
+    hbm = pl.BlockSpec(memory_space=pltpu.HBM)
     flops = 2 * 2 * mats * 2 * rank * rows * width
-    h, c = pl.pallas_call(
+    h, c, held = pl.pallas_call(
         functools.partial(factors_kernel, nb, ns, mats, rank, rows, width, chunk),
         out_shape=(
             jax.ShapeDtypeStruct((mats, 4 * rank, rows), BF16),
             jax.ShapeDtypeStruct((mats, 2 * rank, width), BF16),
-        ),
-        in_specs=[whole, pl.BlockSpec(memory_space=pl.ANY)],
-        out_specs=(whole, whole),
+            jax.ShapeDtypeStruct((mats, rows, width), BF16),
+        ),
+        in_specs=[hbm, hbm],
+        out_specs=(whole, whole, whole),
         scratch_shapes=[
-            vmem((mats, rows, width), BF16),
+            vmem((mats * rank, width), BF16),
             vmem((mats * rank, width), BF16),
             vmem((mats, 2 * rank, width), BF16),
             vmem((mats, 2 * rank, rows), F32),
@@ -243,6 +285,7 @@
             vmem((mats, 2 * rank, 128), F32),
             vmem((mats, ns - 1, 2 * rank, 128), F32),
             vmem((mats, 2 * rank, rows), BF16),
+            vmem((mats, ns if part % 128 else 1, 2 * rank, part), F32),
             vmem((mats, nr, 2 * rank, part), F32),
             vmem((mats, nr, 2 * rank, part), F32),
             vmem((mats, nr - 1, 2 * rank, part), F32),
@@ -252,7 +295,7 @@
             vmem((mats, rank, part), F32),
             vmem((mats, ns, 2 * rank, part), BF16),
             dma((mats, rows // chunk)),
-            dma((2,)),
+            dma((5,)),
             dma((4, mats)),
             dma((mats, ns - 1)),
             dma((mats, ns - 1)),
@@ -263,36 +306,34 @@
             dma((mats, ns - 1)),
         ],
         compiler_params=pltpu.CompilerParams(
-            collective_id=0, has_side_effects=True, vmem_limit_bytes=50 * 2**20
+            collective_id=0, has_side_effects=True, vmem_limit_bytes=16 * 2**20
         ),
         cost_estimate=pl.CostEstimate(
             flops=flops, bytes_accessed=weights.size * 2, transcendentals=0
         ),
         name="factors",
     )(q_warm.reshape(mats * rank, width), weights)
-    step = 1280 if width % 1280 == 0 else width
+    step = 512 if width % 512 == 0 else width
     new_weights, q_next = pl.pallas_call(
-        functools.partial(update_kernel, rank, step),
-        grid=(mats, rows // chunk),
+        functools.partial(update_kernel, rank, tile, step),
         out_shape=(
             jax.ShapeDtypeStruct(weights.shape, BF16),
             jax.ShapeDtypeStruct(q_warm.shape, BF16),
         ),
-        in_specs=[
-            pl.BlockSpec((1, 1, chunk, width), lambda m, t: (0, m, t, 0)),
-            pl.BlockSpec((1, 4 * rank, chunk), lambda m, t: (m, 0, t)),
-            pl.BlockSpec((1, 2 * rank, width), lambda m, t: (m, 0, 0)),
+        in_specs=[whole, whole, whole],
+        out_specs=(hbm, hbm),
+        scratch_shapes=[
+            vmem((3, tile, width), BF16),
+            dma((3,)),
+            vmem((mats, rank, width), BF16),
+            dma((mats,)),
         ],
-        out_specs=(
-            pl.BlockSpec((1, 1, chunk, width), lambda m, t: (0, m, t, 0)),
-            pl.BlockSpec((1, 1, rank, width), lambda m, t: (0, m, 0, 0)),
-        ),
-        compiler_params=pltpu.CompilerParams(vmem_limit_bytes=50 * 2**20),
+        compiler_params=pltpu.CompilerParams(vmem_limit_bytes=16 * 2**20),
         cost_estimate=pl.CostEstimate(
-            flops=flops // 2, bytes_accessed=weights.size * 4, transcendentals=0
+            flops=flops // 2, bytes_accessed=weights.size * 2, transcendentals=0
         ),
         name="update",
-    )(weights, h, c)
+    )(held, h, c)
     return new_weights, q_next
 
 

time: 75.3 us -> 61.2 us (0.81)
  Pallas kernels: 73.4 us -> 59.3 us
    pallas_call x1, Pallas kernels: 23.1 us -> 11.9 us  [per_device(): pl.pallas_call(functools.partial(update_kernel, rank, tile, step), out_sh...]
    pallas_call x1, Pallas kernels: 50.3 us -> 47.4 us  [per_device(): pl.pallas_call(functools.partial(factors_kernel, nb, ns, mats, rank, rows...]
where the time goes in v2:
time: 61.2 us; the launch traced here: 61 us
  Pallas kernels  59.3 us (97%)
  local copies, waits for them, and re-layouts  0.91 us (1%)
  between operations  0.81 us (1%)
    pallas_call x1, Pallas kernels, per_device(): pl.pallas_call(functools.partial(factors_kernel, nb, ns, mats, rank, rows...  47.4 us
    pallas_call x1, Pallas kernels, per_device(): pl.pallas_call(functools.partial(update_kernel, rank, tile, step), out_sh...  11.9 us

profile of v2, /device:TPU:0, one launch (start us, length us, event | category | flops | bytes accessed | tf_op | source)
XLA Modules:
  0.0 61.0 jit_solution(5974473268453919693)
XLA Ops:
  0.6 0.0 copy-start
  0.6 0.9 %copy-done = bf16[1,2,8,5120]{3,2,1,0:T(8,128)(2,1)S(1)} copy-done((bf16[1,2,8,5120]{3,2,1,0:T(8,128)(2,1)S(1)}, bf16[1,2,8,5120]{3,2,1,0:T(8,128)(2,1)}, u32[]{:S(2)}) %copy-start) | copy-done | bytes 163864
  1.5 47.4 %factors.1 = (bf16[2,32,1280]{2,1,0:T(8,128)(2,1)S(1)}, bf16[2,16,5120]{2,1,0:T(8,128)(2,1)S(1)}, bf16[2,1280,5120]{2,1,0:T(8,128)(2,1)S(1)}) custom-call(bf16[16,5120]{1,0:T(8,128)(2,1)S(1)} %bitcast.1, bf16[1,2,1280,5120]{3,2,1,0:T(8,128)(2,1)} %w_ref.1), custom_call_target="tpu_custom_call" | custom-call | flops 838860800 | bytes 26214400 | tf_op jit(solution)/shard_map/factors/pallas_call | solution.py:268
  49.0 11.9 %update.1 = (bf16[1,2,1280,5120]{3,2,1,0:T(8,128)(2,1)}, bf16[1,2,8,5120]{3,2,1,0:T(8,128)(2,1)}) custom-call(bf16[2,1280,5120]{2,1,0:T(8,128)(2,1)S(1)} %get-tuple-element.5.w_ref, bf16[2,32,1280]{2,1,0:T(8,128)(2,1)S(1)} %get-tuple-element.6.h_ref, bf16[2,16,5120]{2,1,0:T(8,128)(2,1)S(1)} %get-tuple-element.7.c_ref), custom_call_target="tpu_custom_call" | custom-call | flops 419430400 | bytes 26214400 | tf_op jit(solution)/shard_map/update/pallas_call | solution.py:317
Async XLA Ops:
  0.6 0.9 %copy-start = (bf16[1,2,8,5120]{3,2,1,0:T(8,128)(2,1)S(1)}, bf16[1,2,8,5120]{3,2,1,0:T(8,128)(2,1)}, u32[]{:S(2)}) copy-start(bf16[1,2,8,5120]{3,2,1,0:T(8,128)(2,1)} %param.3) | copy-start | bytes 491524
